TPU v7x, 128 devices: a whole 4x4x4 slice. The times are simulated.
128 devices in a mesh: group: 8 (over y, core), shard: 16 (over z, x).
Axes of the slice: x: 4, y: 4, z: 4, core: 2. Of those that a mesh axis runs over, the one named last changes fastest.
Arguments:
- queries: bfloat16 [2048, 32, 128], P(('group', 'shard')), may hold values from -12 to 12
- passages: bfloat16 [8192, 64, 128], P(('group', 'shard')), may hold values from -4 to 4
- candidates: int32 [2048, 160], P(('group', 'shard')), may hold values from 0 to 8191, as said below
- passage_slot: int32 [8192], replicated, may hold values from 0 to 8191, as said below
Outputs:
- scores: float32 [2048, 160], P(('group', 'shard'))
Inputs may be any that keep to these rules, and one draw needn't show every extreme that they name: `passage_slot`: every storage row is named by exactly one passage id. `candidates`: candidates k * 20 to (k + 1) * 20 - 1 of a query, for k < 8, all lie in the storage rows of one device, rows d * 64 to (d + 1) * 64 - 1 of device d counted group-major. Over the 16 queries of one device, at most 3 such groups name any one device, and some devices are named exactly 3 times by the queries of every device.
All inputs are finite; a program needn't handle non-finite values.
Results may differ from a plain program's by a relative error of at most 0.0003.
Values may be sent and summed in bfloat16 or wider, within the bound.
A program may use at most 64 MiB of HBM per device.

v0:
```python
import jax
import jax.numpy as jnp
from jax import lax
from jax.sharding import PartitionSpec as P

PER_VISIT = 20


def score_visits(query_rows, local_rows, passages):
    item_count, peer_width, qtok_count, dim_count = query_rows.shape
    slot_count, ptok_count = (passages.shape[0], passages.shape[1])
    visit_total = item_count * peer_width
    block_size = 16
    store_flat = passages.reshape(slot_count * ptok_count, dim_count)
    query_blocks = query_rows.reshape(visit_total // block_size, block_size, qtok_count, dim_count)
    row_blocks = local_rows.reshape(visit_total // block_size, block_size, local_rows.shape[2])
    slot_ids = jnp.arange(slot_count, dtype=jnp.int32)

    def one_block(pieces):
        query_block, row_block = pieces
        similarity = jnp.einsum(
            "vqd,sd->vqs", query_block, store_flat, preferred_element_type=jnp.float32
        )
        best_match = jnp.max(
            similarity.reshape(block_size, qtok_count, slot_count, ptok_count), axis=3
        )
        passage_score = jnp.sum(best_match, axis=1) / qtok_count
        picker = (row_block[:, :, None] == slot_ids[None, None, :]).astype(jnp.float32)
        return jnp.sum(picker * passage_score[:, None, :], axis=2)

    visit_scores = lax.map(one_block, (query_blocks, row_blocks))
    visit_scores = visit_scores.reshape(item_count, peer_width, local_rows.shape[2])
    return lax.all_to_all(visit_scores, ("group", "shard"), split_axis=1, concat_axis=1, tiled=True)


def local(queries, passages, candidates, passage_slot):
    peer_count = lax.axis_size(("group", "shard"))
    query_count, cand_count = candidates.shape
    slot_count = passages.shape[0]
    spread_count = cand_count // PER_VISIT
    capacity = 3 * query_count * spread_count // peer_count
    visit_count = query_count * spread_count
    storage = passage_slot[candidates].reshape(visit_count, PER_VISIT)
    target = storage[:, 0] // slot_count
    local_rows = storage % slot_count
    matches = (target[:, None] == jnp.arange(peer_count, dtype=jnp.int32)[None, :]).astype(
        jnp.int32
    )
    before = jnp.cumsum(matches, axis=0) - matches
    rank_in = jnp.sum(before * matches, axis=1)
    position = rank_in * peer_count + target
    holder = (
        jnp.zeros((capacity * peer_count,), jnp.int32)
        .at[position]
        .set(jnp.arange(visit_count, dtype=jnp.int32))
    )
    send_local = local_rows[holder].reshape(capacity, peer_count, PER_VISIT)
    query_local = holder // spread_count
    everyone = lax.all_gather(queries, ("group", "shard"), axis=0, tiled=True)
    query_global = (lax.axis_index(("group", "shard")) * query_count + query_local).reshape(
        capacity, peer_count
    )
    wanted = lax.all_to_all(
        query_global, ("group", "shard"), split_axis=1, concat_axis=1, tiled=True
    )
    local_block = lax.all_to_all(
        send_local, ("group", "shard"), split_axis=1, concat_axis=1, tiled=True
    )
    returned = score_visits(everyone[wanted], local_block, passages)
    flat_scores = returned.reshape(capacity * peer_count, PER_VISIT)[position]
    return flat_scores.reshape(query_count, cand_count)


def solution(mesh):
    return jax.shard_map(
        local,
        mesh=mesh,
        in_specs=(
            P(("group", "shard"), None, None),
            P(("group", "shard"), None, None),
            P(("group", "shard"), None),
            P(),
        ),
        out_specs=P(("group", "shard"), None),
        check_vma=False,
    )
```

profile of v0, /device:TPU:1, one launch (start us, length us, event | category | flops | bytes accessed | tf_op | source)
XLA Modules:
  0.0 281.4 jit_solution(6359539791952845427)
XLA Ops:
  8.1 13.6 %gather_fusion = s32[2560]{0:T(1024)S(1)} fusion(s32[8192]{0:T(1024)S(1)} %copy-done, s32[3072]{0:T(1024)S(1)} %pad_clamp_fusion), kind=kCustom, calls=%fused_computation | custom fusion | bytes 30720 | tf_op jit(solution)/shard_map/gather | solution.py:43
  24.4 11.5 %all-to-all-start.1 = ((s32[3,128,1]{0,2,1:T(1,128)}), s32[3,128,1]{0,2,1:T(1,128)S(1)}, u32[]{:S(2)}, u32[]{:S(2)}) async-start(s32[3,128,1]{0,2,1:T(1,128)} %copy.34), calls=%async_computation.1 | async-start | bytes 131072 | tf_op jit(solution)/shard_map/all_to_all | solution.py:63
  37.9 7.7 %all-to-all-done.1 = s32[3,128,1]{0,2,1:T(1,128)S(1)} async-done(((s32[3,128,1]{0,2,1:T(1,128)}), s32[3,128,1]{0,2,1:T(1,128)S(1)}, u32[]{:S(2)}, u32[]{:S(2)}) %all-to-all-start.1) | async-done | bytes 1568 | tf_op jit(solution)/shard_map/all_to_all | solution.py:63
  50.1 12.4 %all-to-all-done = s32[3,128,20]{2,0,1:T(4,128)S(1)} async-done(((s32[3,128,20]{2,0,1:T(4,128)}), s32[3,128,20]{2,0,1:T(4,128)S(1)}, u32[]{:S(2)}, u32[]{:S(2)}) %all-to-all-start) | async-done | bytes 30752 | tf_op jit(solution)/shard_map/all_to_all | solution.py:66
  62.6 34.5 %all-gather.2.cloned.1.call-done = bf16[2048,32,128]{2,1,0:T(8,128)(2,1)} async-done(((bf16[16,32,128]{2,1,0:T(8,128)(2,1)}), bf16[2048,32,128]{2,1,0:T(8,128)(2,1)}) %all-gather.2.cloned.1.call-update) | async-done | bytes 16777232 | tf_op jit(solution)/shard_map/all_gather | solution.py:59
  97.1 8.5 %gather_fusion.2 = bf16[384,32,128]{2,1,0:T(8,128)(2,1)} fusion(bf16[2048,32,128]{2,1,0:T(8,128)(2,1)} %all-gather.2.cloned.1.call-done, s32[1024]{0:T(1024)S(1)} %pad_clamp_fusion.2), kind=kCustom, calls=%fused_computation.2 | custom fusion | bytes 6292992 | tf_op jit(solution)/shard_map/gather | solution.py:69
  105.5 148.0 %while.11 = (s32[]{:T(128)}, f32[24,16,20]{2,1,0:T(8,128)S(1)}, s32[24,16,20]{2,1,0:T(8,128)S(1)}, bf16[24,16,32,128]{3,2,1,0:T(8,128)(2,1)}, bf16[4096,128]{1,0:T(8,128)(2,1)S(1)}, /*index=5*/s32[]{:T(128)}, f32[]{:T(128)}) while((s32[]{:T(128)}, f32[24,16,20]{2,1,0:T(8,128)S(1)}, s32[24,16,20]{2,1,0:T(8,128)S(1)}, ...), condition=%wide.region_7.8_spmd.clone, body=%wide.region_3.7_spmd.clone.sunk | while | flops 539029184 | bytes 1484901 | solution.py:31
  105.6 5.6 %convolution_reduce_fusion.2 = f32[16,32,64]{1,2,0:T(8,128)S(1)} fusion(bf16[64,64,128,1]{2,1,0,3:T(8,128)(2,1)S(1)} %bitcast.43, bf16[24,16,32,128]{3,2,1,0:T(8,128)(2,1)} %get-tuple-element.130, s32[]{:T(128)S(6)} %copy.52), kind=kOutput, calls=%fused_computation.6.clone.1 | convolution fusion | flops 538935296 | bytes 1310724 | tf_op jit(solution)/shard_map/while/body/eval_jaxpr/vqd,sd->vqs/dot_general | solution.py:21
  111.8 5.6 %convolution_reduce_fusion.2 = f32[16,32,64]{1,2,0:T(8,128)S(1)} fusion(bf16[64,64,128,1]{2,1,0,3:T(8,128)(2,1)S(1)} %bitcast.43, bf16[24,16,32,128]{3,2,1,0:T(8,128)(2,1)} %get-tuple-element.130, s32[]{:T(128)S(6)} %copy.52), kind=kOutput, calls=%fused_computation.6.clone.1 | convolution fusion | flops 538935296 | bytes 1310724 | tf_op jit(solution)/shard_map/while/body/eval_jaxpr/vqd,sd->vqs/dot_general | solution.py:21
  118.0 5.5 %convolution_reduce_fusion.2 = f32[16,32,64]{1,2,0:T(8,128)S(1)} fusion(bf16[64,64,128,1]{2,1,0,3:T(8,128)(2,1)S(1)} %bitcast.43, bf16[24,16,32,128]{3,2,1,0:T(8,128)(2,1)} %get-tuple-element.130, s32[]{:T(128)S(6)} %copy.52), kind=kOutput, calls=%fused_computation.6.clone.1 | convolution fusion | flops 538935296 | bytes 1310724 | tf_op jit(solution)/shard_map/while/body/eval_jaxpr/vqd,sd->vqs/dot_general | solution.py:21
  124.1 5.6 %convolution_reduce_fusion.2 = f32[16,32,64]{1,2,0:T(8,128)S(1)} fusion(bf16[64,64,128,1]{2,1,0,3:T(8,128)(2,1)S(1)} %bitcast.43, bf16[24,16,32,128]{3,2,1,0:T(8,128)(2,1)} %get-tuple-element.130, s32[]{:T(128)S(6)} %copy.52), kind=kOutput, calls=%fused_computation.6.clone.1 | convolution fusion | flops 538935296 | bytes 1310724 | tf_op jit(solution)/shard_map/while/body/eval_jaxpr/vqd,sd->vqs/dot_general | solution.py:21
  130.3 5.6 %convolution_reduce_fusion.2 = f32[16,32,64]{1,2,0:T(8,128)S(1)} fusion(bf16[64,64,128,1]{2,1,0,3:T(8,128)(2,1)S(1)} %bitcast.43, bf16[24,16,32,128]{3,2,1,0:T(8,128)(2,1)} %get-tuple-element.130, s32[]{:T(128)S(6)} %copy.52), kind=kOutput, calls=%fused_computation.6.clone.1 | convolution fusion | flops 538935296 | bytes 1310724 | tf_op jit(solution)/shard_map/while/body/eval_jaxpr/vqd,sd->vqs/dot_general | solution.py:21
  136.5 5.5 %convolution_reduce_fusion.2 = f32[16,32,64]{1,2,0:T(8,128)S(1)} fusion(bf16[64,64,128,1]{2,1,0,3:T(8,128)(2,1)S(1)} %bitcast.43, bf16[24,16,32,128]{3,2,1,0:T(8,128)(2,1)} %get-tuple-element.130, s32[]{:T(128)S(6)} %copy.52), kind=kOutput, calls=%fused_computation.6.clone.1 | convolution fusion | flops 538935296 | bytes 1310724 | tf_op jit(solution)/shard_map/while/body/eval_jaxpr/vqd,sd->vqs/dot_general | solution.py:21
  142.6 5.6 %convolution_reduce_fusion.2 = f32[16,32,64]{1,2,0:T(8,128)S(1)} fusion(bf16[64,64,128,1]{2,1,0,3:T(8,128)(2,1)S(1)} %bitcast.43, bf16[24,16,32,128]{3,2,1,0:T(8,128)(2,1)} %get-tuple-element.130, s32[]{:T(128)S(6)} %copy.52), kind=kOutput, calls=%fused_computation.6.clone.1 | convolution fusion | flops 538935296 | bytes 1310724 | tf_op jit(solution)/shard_map/while/body/eval_jaxpr/vqd,sd->vqs/dot_general | solution.py:21
  148.8 5.6 %convolution_reduce_fusion.2 = f32[16,32,64]{1,2,0:T(8,128)S(1)} fusion(bf16[64,64,128,1]{2,1,0,3:T(8,128)(2,1)S(1)} %bitcast.43, bf16[24,16,32,128]{3,2,1,0:T(8,128)(2,1)} %get-tuple-element.130, s32[]{:T(128)S(6)} %copy.52), kind=kOutput, calls=%fused_computation.6.clone.1 | convolution fusion | flops 538935296 | bytes 1310724 | tf_op jit(solution)/shard_map/while/body/eval_jaxpr/vqd,sd->vqs/dot_general | solution.py:21
  155.0 5.5 %convolution_reduce_fusion.2 = f32[16,32,64]{1,2,0:T(8,128)S(1)} fusion(bf16[64,64,128,1]{2,1,0,3:T(8,128)(2,1)S(1)} %bitcast.43, bf16[24,16,32,128]{3,2,1,0:T(8,128)(2,1)} %get-tuple-element.130, s32[]{:T(128)S(6)} %copy.52), kind=kOutput, calls=%fused_computation.6.clone.1 | convolution fusion | flops 538935296 | bytes 1310724 | tf_op jit(solution)/shard_map/while/body/eval_jaxpr/vqd,sd->vqs/dot_general | solution.py:21
  161.1 5.6 %convolution_reduce_fusion.2 = f32[16,32,64]{1,2,0:T(8,128)S(1)} fusion(bf16[64,64,128,1]{2,1,0,3:T(8,128)(2,1)S(1)} %bitcast.43, bf16[24,16,32,128]{3,2,1,0:T(8,128)(2,1)} %get-tuple-element.130, s32[]{:T(128)S(6)} %copy.52), kind=kOutput, calls=%fused_computation.6.clone.1 | convolution fusion | flops 538935296 | bytes 1310724 | tf_op jit(solution)/shard_map/while/body/eval_jaxpr/vqd,sd->vqs/dot_general | solution.py:21
  167.3 5.6 %convolution_reduce_fusion.2 = f32[16,32,64]{1,2,0:T(8,128)S(1)} fusion(bf16[64,64,128,1]{2,1,0,3:T(8,128)(2,1)S(1)} %bitcast.43, bf16[24,16,32,128]{3,2,1,0:T(8,128)(2,1)} %get-tuple-element.130, s32[]{:T(128)S(6)} %copy.52), kind=kOutput, calls=%fused_computation.6.clone.1 | convolution fusion | flops 538935296 | bytes 1310724 | tf_op jit(solution)/shard_map/while/body/eval_jaxpr/vqd,sd->vqs/dot_general | solution.py:21
  173.5 5.5 %convolution_reduce_fusion.2 = f32[16,32,64]{1,2,0:T(8,128)S(1)} fusion(bf16[64,64,128,1]{2,1,0,3:T(8,128)(2,1)S(1)} %bitcast.43, bf16[24,16,32,128]{3,2,1,0:T(8,128)(2,1)} %get-tuple-element.130, s32[]{:T(128)S(6)} %copy.52), kind=kOutput, calls=%fused_computation.6.clone.1 | convolution fusion | flops 538935296 | bytes 1310724 | tf_op jit(solution)/shard_map/while/body/eval_jaxpr/vqd,sd->vqs/dot_general | solution.py:21
  179.6 5.6 %convolution_reduce_fusion.2 = f32[16,32,64]{1,2,0:T(8,128)S(1)} fusion(bf16[64,64,128,1]{2,1,0,3:T(8,128)(2,1)S(1)} %bitcast.43, bf16[24,16,32,128]{3,2,1,0:T(8,128)(2,1)} %get-tuple-element.130, s32[]{:T(128)S(6)} %copy.52), kind=kOutput, calls=%fused_computation.6.clone.1 | convolution fusion | flops 538935296 | bytes 1310724 | tf_op jit(solution)/shard_map/while/body/eval_jaxpr/vqd,sd->vqs/dot_general | solution.py:21
  185.8 5.6 %convolution_reduce_fusion.2 = f32[16,32,64]{1,2,0:T(8,128)S(1)} fusion(bf16[64,64,128,1]{2,1,0,3:T(8,128)(2,1)S(1)} %bitcast.43, bf16[24,16,32,128]{3,2,1,0:T(8,128)(2,1)} %get-tuple-element.130, s32[]{:T(128)S(6)} %copy.52), kind=kOutput, calls=%fused_computation.6.clone.1 | convolution fusion | flops 538935296 | bytes 1310724 | tf_op jit(solution)/shard_map/while/body/eval_jaxpr/vqd,sd->vqs/dot_general | solution.py:21
  192.0 5.5 %convolution_reduce_fusion.2 = f32[16,32,64]{1,2,0:T(8,128)S(1)} fusion(bf16[64,64,128,1]{2,1,0,3:T(8,128)(2,1)S(1)} %bitcast.43, bf16[24,16,32,128]{3,2,1,0:T(8,128)(2,1)} %get-tuple-element.130, s32[]{:T(128)S(6)} %copy.52), kind=kOutput, calls=%fused_computation.6.clone.1 | convolution fusion | flops 538935296 | bytes 1310724 | tf_op jit(solution)/shard_map/while/body/eval_jaxpr/vqd,sd->vqs/dot_general | solution.py:21
  198.1 5.6 %convolution_reduce_fusion.2 = f32[16,32,64]{1,2,0:T(8,128)S(1)} fusion(bf16[64,64,128,1]{2,1,0,3:T(8,128)(2,1)S(1)} %bitcast.43, bf16[24,16,32,128]{3,2,1,0:T(8,128)(2,1)} %get-tuple-element.130, s32[]{:T(128)S(6)} %copy.52), kind=kOutput, calls=%fused_computation.6.clone.1 | convolution fusion | flops 538935296 | bytes 1310724 | tf_op jit(solution)/shard_map/while/body/eval_jaxpr/vqd,sd->vqs/dot_general | solution.py:21
  204.3 5.6 %convolution_reduce_fusion.2 = f32[16,32,64]{1,2,0:T(8,128)S(1)} fusion(bf16[64,64,128,1]{2,1,0,3:T(8,128)(2,1)S(1)} %bitcast.43, bf16[24,16,32,128]{3,2,1,0:T(8,128)(2,1)} %get-tuple-element.130, s32[]{:T(128)S(6)} %copy.52), kind=kOutput, calls=%fused_computation.6.clone.1 | convolution fusion | flops 538935296 | bytes 1310724 | tf_op jit(solution)/shard_map/while/body/eval_jaxpr/vqd,sd->vqs/dot_general | solution.py:21
  210.5 5.5 %convolution_reduce_fusion.2 = f32[16,32,64]{1,2,0:T(8,128)S(1)} fusion(bf16[64,64,128,1]{2,1,0,3:T(8,128)(2,1)S(1)} %bitcast.43, bf16[24,16,32,128]{3,2,1,0:T(8,128)(2,1)} %get-tuple-element.130, s32[]{:T(128)S(6)} %copy.52), kind=kOutput, calls=%fused_computation.6.clone.1 | convolution fusion | flops 538935296 | bytes 1310724 | tf_op jit(solution)/shard_map/while/body/eval_jaxpr/vqd,sd->vqs/dot_general | solution.py:21
  216.6 5.6 %convolution_reduce_fusion.2 = f32[16,32,64]{1,2,0:T(8,128)S(1)} fusion(bf16[64,64,128,1]{2,1,0,3:T(8,128)(2,1)S(1)} %bitcast.43, bf16[24,16,32,128]{3,2,1,0:T(8,128)(2,1)} %get-tuple-element.130, s32[]{:T(128)S(6)} %copy.52), kind=kOutput, calls=%fused_computation.6.clone.1 | convolution fusion | flops 538935296 | bytes 1310724 | tf_op jit(solution)/shard_map/while/body/eval_jaxpr/vqd,sd->vqs/dot_general | solution.py:21
  222.8 5.6 %convolution_reduce_fusion.2 = f32[16,32,64]{1,2,0:T(8,128)S(1)} fusion(bf16[64,64,128,1]{2,1,0,3:T(8,128)(2,1)S(1)} %bitcast.43, bf16[24,16,32,128]{3,2,1,0:T(8,128)(2,1)} %get-tuple-element.130, s32[]{:T(128)S(6)} %copy.52), kind=kOutput, calls=%fused_computation.6.clone.1 | convolution fusion | flops 538935296 | bytes 1310724 | tf_op jit(solution)/shard_map/while/body/eval_jaxpr/vqd,sd->vqs/dot_general | solution.py:21
  235.1 5.6 %convolution_reduce_fusion.2 = f32[16,32,64]{1,2,0:T(8,128)S(1)} fusion(bf16[64,64,128,1]{2,1,0,3:T(8,128)(2,1)S(1)} %bitcast.43, bf16[24,16,32,128]{3,2,1,0:T(8,128)(2,1)} %get-tuple-element.130, s32[]{:T(128)S(6)} %copy.52), kind=kOutput, calls=%fused_computation.6.clone.1 | convolution fusion | flops 538935296 | bytes 1310724 | tf_op jit(solution)/shard_map/while/body/eval_jaxpr/vqd,sd->vqs/dot_general | solution.py:21
  241.3 5.6 %convolution_reduce_fusion.2 = f32[16,32,64]{1,2,0:T(8,128)S(1)} fusion(bf16[64,64,128,1]{2,1,0,3:T(8,128)(2,1)S(1)} %bitcast.43, bf16[24,16,32,128]{3,2,1,0:T(8,128)(2,1)} %get-tuple-element.130, s32[]{:T(128)S(6)} %copy.52), kind=kOutput, calls=%fused_computation.6.clone.1 | convolution fusion | flops 538935296 | bytes 1310724 | tf_op jit(solution)/shard_map/while/body/eval_jaxpr/vqd,sd->vqs/dot_general | solution.py:21
  247.5 5.5 %convolution_reduce_fusion.2 = f32[16,32,64]{1,2,0:T(8,128)S(1)} fusion(bf16[64,64,128,1]{2,1,0,3:T(8,128)(2,1)S(1)} %bitcast.43, bf16[24,16,32,128]{3,2,1,0:T(8,128)(2,1)} %get-tuple-element.130, s32[]{:T(128)S(6)} %copy.52), kind=kOutput, calls=%fused_computation.6.clone.1 | convolution fusion | flops 538935296 | bytes 1310724 | tf_op jit(solution)/shard_map/while/body/eval_jaxpr/vqd,sd->vqs/dot_general | solution.py:21
  254.4 7.3 %all-to-all-start.2 = ((f32[3,128,20]{2,0,1:T(4,128)}), f32[3,128,20]{2,0,1:T(4,128)S(1)}, u32[]{:S(2)}, u32[]{:S(2)}) async-start(f32[3,128,20]{2,0,1:T(4,128)} %copy.38), calls=%async_computation.2 | async-start | bytes 524288 | tf_op jit(solution)/shard_map/all_to_all | solution.py:33
  261.7 11.5 %all-to-all-done.2 = f32[3,128,20]{2,0,1:T(4,128)S(1)} async-done(((f32[3,128,20]{2,0,1:T(4,128)}), f32[3,128,20]{2,0,1:T(4,128)S(1)}, u32[]{:S(2)}, u32[]{:S(2)}) %all-to-all-start.2) | async-done | bytes 30752 | tf_op jit(solution)/shard_map/all_to_all | solution.py:33
  (205 shorter events, 32.4 us)
Async XLA Ops:
  6.5 1.5 copy-start
  6.5 90.5 %all-gather.2.cloned.1.call-start = ((), (), s32[]{:S(2)}) async-start(), calls=%async_computation.3 | async-start | bytes 16908288 | tf_op jit(solution)/shard_map/all_gather | solution.py:59
  24.4 21.3 %all-to-all-start.1 = ((s32[3,128,1]{0,2,1:T(1,128)}), s32[3,128,1]{0,2,1:T(1,128)S(1)}, u32[]{:S(2)}, u32[]{:S(2)}) async-start(s32[3,128,1]{0,2,1:T(1,128)} %copy.34), calls=%async_computation.1 | async-start | bytes 131072 | tf_op jit(solution)/shard_map/all_to_all | solution.py:63
  45.7 16.9 %all-to-all-start = ((s32[3,128,20]{2,0,1:T(4,128)}), s32[3,128,20]{2,0,1:T(4,128)S(1)}, u32[]{:S(2)}, u32[]{:S(2)}) async-start(s32[3,128,20]{2,0,1:T(4,128)} %copy.32), calls=%async_computation | async-start | bytes 524288 | tf_op jit(solution)/shard_map/all_to_all | solution.py:66
  62.5 43.0 %copy-start.1 = (bf16[64,64,128]{2,1,0:T(8,128)(2,1)S(1)}, bf16[64,64,128]{2,1,0:T(8,128)(2,1)}, u32[]{:S(2)}) copy-start(bf16[64,64,128]{2,1,0:T(8,128)(2,1)} %param.7) | copy-start | bytes 3145732
  254.4 18.8 %all-to-all-start.2 = ((f32[3,128,20]{2,0,1:T(4,128)}), f32[3,128,20]{2,0,1:T(4,128)S(1)}, u32[]{:S(2)}, u32[]{:S(2)}) async-start(f32[3,128,20]{2,0,1:T(4,128)} %copy.38), calls=%async_computation.2 | async-start | bytes 524288 | tf_op jit(solution)/shard_map/all_to_all | solution.py:33
Sparse Core Ops, SparseCore 0:
  10.5 86.5 all-gather.1
where the time goes:
time: 282 us; the launch traced here: 281 us
  matrix products  133 us (47%)
  waiting for transfers between devices  66.8 us (24%)
  local copies, waits for them, and re-layouts  32.5 us (12%)
  starting transfers between devices  23.1 us (8%)
  between operations  13.6 us (5%)
  other arithmetic  11.5 us (4%)
    dot_general x24, matrix products, one_block(): jnp.einsum('vqd,sd->vqs', query_block, store_flat, preferred_element_type...  133 us
    all_gather x1, waiting for transfers between devices, local(): everyone = lax.all_gather(queries, ('group', 'shard'), axis=0, tiled=True)  34.5 us
    gather x1, local copies, waits for them, and re-layouts, local(): storage = passage_slot[candidates].reshape(visit_count, PER_VISIT)  13.6 us
    all_to_all x1, waiting for transfers between devices, local(): lax.all_to_all(send_local, ('group', 'shard'), split_axis=1, concat_axis=...  12.4 us
    all_to_all x1, starting transfers between devices, local(): lax.all_to_all(query_global, ('group', 'shard'), split_axis=1, concat_axi...  11.5 us
    all_to_all x1, waiting for transfers between devices, score_visits(): lax.all_to_all(visit_scores, ('group', 'shard'), split_axis=1, concat_axi...  11.5 us
    gather x1, local copies, waits for them, and re-layouts, local(): returned = score_visits(everyone[wanted], local_block, passages)  8.47 us
    all_to_all x1, waiting for transfers between devices, local(): lax.all_to_all(query_global, ('group', 'shard'), split_axis=1, concat_axi...  7.74 us
  transfers between devices with their start and end apart: 4, of which 4 were waited for; matrix products, arithmetic and copies ran while one was open for 7% of the time, Pallas kernels for 0%

commit v1 on v0

v1 whole, which is shorter than its diff:
```python
import functools

import jax
import jax.numpy as jnp
from jax import lax
from jax.experimental import pallas as pl
from jax.experimental.pallas import tpu as pltpu
from jax.sharding import PartitionSpec as P

PER_VISIT = 20
SPREAD = 8
CAP = 3
PEERS = 128
CHUNK = 16
MESH = pl.DeviceIdType.MESH


def offset_target(y, c, z, x, o, sign):
    i, j = o // 32, (o // 8) % 4
    dx, dc = (o // 2) % 4, o % 2
    dz = (j % 2) * 2 + j // 2
    dy = (i + dz + dx) % 4
    ty = (y + sign * dy + 4) % 4
    tz = (z + sign * dz + 4) % 4
    tx = (x + sign * dx + 4) % 4
    tc = (c + dc) % 2
    group, shard = ty * 2 + tc, tz * 4 + tx
    return group, shard, group * 16 + shard


def kernel(
    q_ref, p_ref, cand_ref, slot_ref, out_ref,
    send, recv, pt, p32, retsend, ret, picked, route, route_s,
    send_sem, recv_sem, retsend_sem, ret_sem, local_sem,
):
    group, shard = lax.axis_index("group"), lax.axis_index("shard")
    y, c, z, x = group // 2, group % 2, shard // 4, shard % 4
    me = group * 16 + shard
    qn, tok, dim = q_ref.shape
    rows = CAP * tok

    cand = cand_ref[...]
    wide = jnp.concatenate(
        [jnp.pad(cand[:, k * PER_VISIT:(k + 1) * PER_VISIT], ((0, 0), (0, 128 - PER_VISIT)))
         for k in range(SPREAD)], axis=0)
    cand_t = wide.T[:24]
    hi, lo = cand_t // 128, cand_t % 128
    storage = jnp.zeros((24, 128), jnp.int32)
    for h in range(64):
        line = jnp.broadcast_to(slot_ref[h:h + 1, :], (24, 128))
        storage = jnp.where(hi == h, jnp.take_along_axis(line, lo, axis=1), storage)
    local_rows = jnp.pad(storage % 64, ((0, 104), (0, 0))).T
    target = storage[0:1, :] // 64

    down = lax.broadcasted_iota(jnp.int32, (128, 128), 0)
    across = lax.broadcasted_iota(jnp.int32, (128, 128), 1)
    matches = down == target
    matches_b = jnp.where(matches, 1.0, 0.0).astype(jnp.bfloat16)
    upper = jnp.where(down < across, 1.0, 0.0).astype(jnp.bfloat16)
    before = jnp.dot(matches_b, upper, preferred_element_type=jnp.float32)
    rank = jnp.sum(jnp.where(matches, before, 0.0), axis=0, keepdims=True)
    query = (lax.broadcasted_iota(jnp.int32, (8, 128), 1) % qn).astype(jnp.float32)
    level = lax.broadcasted_iota(jnp.int32, (8, 128), 0).astype(jnp.float32)
    held = jnp.where(level == rank, query, 0.0).astype(jnp.bfloat16)
    slots = lax.dot_general(held, matches_b, (((1,), (1,)), ((), ())), preferred_element_type=jnp.float32)
    route[0:8, :] = jnp.clip(slots.astype(jnp.int32), 0, qn - 1)
    route[8:16, :] = jnp.broadcast_to(jnp.clip(target, 0, PEERS - 1), (8, 128))
    route[16:24, :] = jnp.broadcast_to(jnp.clip(rank.astype(jnp.int32), 0, CAP - 1), (8, 128))
    copy = pltpu.make_async_copy(route, route_s, local_sem)
    copy.start()
    copy.wait()

    def fill(ref, o, number):
        for r in range(CAP):
            ref[pl.ds(o * rows + r * tok, tok), :] = q_ref[route_s[r, number]]

    fill(recv, 0, me)

    @pl.loop(1, PEERS)
    def _(o):
        tg, ts, number = offset_target(y, c, z, x, o, 1)
        fill(send, o, number)
        pltpu.make_async_remote_copy(
            src_ref=send.at[pl.ds(o * rows, rows), :],
            dst_ref=recv.at[pl.ds(o * rows, rows), :],
            send_sem=send_sem,
            recv_sem=recv_sem.at[o // CHUNK],
            device_id=(tg, ts),
            device_id_type=MESH,
        ).start()

    p32[...] = p_ref[...].reshape(p32.shape).astype(jnp.float32)
    for t in range(64):
        pt[t * 64:(t + 1) * 64, :] = p32[pl.ds(t, 64, stride=64), :].astype(jnp.bfloat16)

    def score(k):
        lhs = recv[pl.ds(k * CHUNK * rows, CHUNK * rows), :]
        best = None
        for n in range(16):
            sim = lax.dot_general(
                lhs, pt[n * 256:(n + 1) * 256, :], (((1,), (1,)), ((), ())),
                preferred_element_type=jnp.float32)
            two = jnp.maximum(sim[:, :128], sim[:, 128:])
            best = two if best is None else jnp.maximum(best, two)
        best = jnp.maximum(best, pltpu.roll(best, 64, 1))
        return jnp.sum(best.reshape(CHUNK * CAP, tok, 128), axis=1) * (1.0 / tok)

    @pl.loop(0, PEERS // CHUNK)
    def _(k):
        @pl.when(k == 0)
        def _():
            part = recv.at[pl.ds(rows, (CHUNK - 1) * rows), :]
            pltpu.make_async_copy(part, part, recv_sem.at[0]).wait()

        @pl.when(k > 0)
        def _():
            part = recv.at[pl.ds(k * CHUNK * rows, CHUNK * rows), :]
            pltpu.make_async_copy(part, part, recv_sem.at[k]).wait()

        total = score(k)
        for j in range(CHUNK):
            retsend[k * CHUNK + j, 0:CAP, :] = total[j * CAP:(j + 1) * CAP, :]

        @pl.loop(0, CHUNK)
        def _(j):
            o = k * CHUNK + j

            @pl.when(o > 0)
            def _():
                tg, ts, number = offset_target(y, c, z, x, o, -1)
                pltpu.make_async_remote_copy(
                    src_ref=retsend.at[o],
                    dst_ref=ret.at[me],
                    send_sem=retsend_sem,
                    recv_sem=ret_sem,
                    device_id=(tg, ts),
                    device_id_type=MESH,
                ).start()

            @pl.when(o == 0)
            def _():
                ret[me] = retsend[0]

    part = retsend.at[pl.ds(1, PEERS - 1)]
    pltpu.make_async_copy(part, part, ret_sem).wait()

    @pl.loop(0, PEERS)
    def _(v):
        picked[pl.ds(v, 1), :] = ret[route_s[8, v], pl.ds(route_s[16, v], 1), :]

    scores = jnp.take_along_axis(picked[...], local_rows, axis=1)
    for k in range(SPREAD):
        out_ref[:, k * PER_VISIT:(k + 1) * PER_VISIT] = scores[k * qn:(k + 1) * qn, :PER_VISIT]

    pltpu.make_async_copy(part, part, retsend_sem).wait()
    part = send.at[pl.ds(rows, (PEERS - 1) * rows), :]
    pltpu.make_async_copy(part, part, send_sem).wait()


def local(queries, passages, candidates, passage_slot):
    rows = CAP * queries.shape[1]
    dim = queries.shape[2]
    return pl.pallas_call(
        kernel,
        out_shape=jax.ShapeDtypeStruct(candidates.shape, jnp.float32),
        in_specs=[pl.BlockSpec(memory_space=pltpu.VMEM)] * 4,
        out_specs=pl.BlockSpec(memory_space=pltpu.VMEM),
        scratch_shapes=[
            pltpu.VMEM((PEERS * rows, dim), jnp.bfloat16),
            pltpu.VMEM((PEERS * rows, dim), jnp.bfloat16),
            pltpu.VMEM((4096, dim), jnp.bfloat16),
            pltpu.VMEM((4096, dim), jnp.float32),
            pltpu.VMEM((PEERS, 8, 128), jnp.float32),
            pltpu.VMEM((PEERS, 8, 128), jnp.float32),
            pltpu.VMEM((PEERS, 128), jnp.float32),
            pltpu.VMEM((24, 128), jnp.int32),
            pltpu.SMEM((24, 128), jnp.int32),
            pltpu.SemaphoreType.DMA,
            pltpu.SemaphoreType.DMA((PEERS // CHUNK,)),
            pltpu.SemaphoreType.DMA,
            pltpu.SemaphoreType.DMA,
            pltpu.SemaphoreType.DMA,
        ],
        compiler_params=pltpu.CompilerParams(
            has_side_effects=True, vmem_limit_bytes=52 * 2**20),
    )(queries, passages, candidates, passage_slot.reshape(64, 128))


def solution(mesh):
    return jax.shard_map(
        local,
        mesh=mesh,
        in_specs=(
            P(("group", "shard"), None, None),
            P(("group", "shard"), None, None),
            P(("group", "shard"), None),
            P(),
        ),
        out_specs=P(("group", "shard"), None),
        check_vma=False,
    )
```

time: 282 us -> 86.1 us (0.31)
  matrix products: 133 us -> 0 us
  Pallas kernels: 0 us -> 81.6 us
  waiting for transfers between devices: 66.8 us -> 0 us
  local copies, waits for them, and re-layouts: 32.5 us -> 4.21 us
  starting transfers between devices: 23.1 us -> 0 us
  between operations: 13.6 us -> 0.01 us
  other arithmetic: 11.5 us -> 0 us
    dot_general x24 -> x0, matrix products: 133 us -> none  [one_block(): jnp.einsum('vqd,sd->vqs', query_block, store_flat, preferred_element_type...]
    pallas_call x0 -> x1, Pallas kernels: none -> 81.6 us  [local(): pl.pallas_call(kernel, out_shape=jax.ShapeDtypeStruct(candidates.shape, j...]
    all_gather x1 -> x0, waiting for transfers between devices: 34.5 us -> none  [local(): everyone = lax.all_gather(queries, ('group', 'shard'), axis=0, tiled=True)]
    all_to_all x3 -> x0, waiting for transfers between devices: 31.6 us -> none  [the longest x1 12.4 us: local(): lax.all_to_all(send_local, ('group', 'shard'), split_axis=1, concat_axis=...]
    gather x4 -> x0, local copies, waits for them, and re-layouts: 23.9 us -> none  [the longest x1 13.6 us: local(): storage = passage_slot[candidates].reshape(visit_count, PER_VISIT)]
    all_to_all x3 -> x0, starting transfers between devices: 23.1 us -> none  [the longest x1 11.5 us: local(): lax.all_to_all(query_global, ('group', 'shard'), split_axis=1, concat_axi...]
    reduce_sum x49 -> x0, other arithmetic: 10 us -> none  [the longest x24 5.03 us: one_block(): passage_score = jnp.sum(best_match, axis=1) / qtok_count]
    unnamed x5 -> x9, local copies, waits for them, and re-layouts: 0.02 us -> 4.21 us
  transfers between devices with their start and end apart: 4 -> 0, of which waited for: 4 -> 0; matrix products, arithmetic and copies ran while one was open for 7% -> 0% of each run, Pallas kernels for 0% -> 0%
where the time goes in v1:
time: 86.1 us; the launch traced here: 85.8 us
  Pallas kernels  81.6 us (95%)
  local copies, waits for them, and re-layouts  4.21 us (5%)
    pallas_call x1, Pallas kernels, local(): pl.pallas_call(kernel, out_shape=jax.ShapeDtypeStruct(candidates.shape, j...  81.6 us
    unnamed x9, local copies, waits for them, and re-layouts  4.21 us

profile of v1, /device:TPU:1, one launch (start us, length us, event | category | flops | bytes accessed | tf_op | source)
XLA Modules:
  0.0 85.8 jit_solution(8986762239231343550)
XLA Ops:
  0.0 0.0 copy-start
  0.0 1.2 %copy-done = bf16[64,64,128]{2,1,0:T(8,128)(2,1)S(1)} copy-done((bf16[64,64,128]{2,1,0:T(8,128)(2,1)S(1)}, bf16[64,64,128]{2,1,0:T(8,128)(2,1)}, u32[]{:S(2)}) %copy-start) | copy-done | bytes 1048600
  1.2 0.0 copy-start.1
  1.2 0.9 %copy-done.1 = bf16[16,32,128]{2,1,0:T(8,128)(2,1)S(1)} copy-done((bf16[16,32,128]{2,1,0:T(8,128)(2,1)S(1)}, bf16[16,32,128]{2,1,0:T(8,128)(2,1)}, u32[]{:S(2)}) %copy-start.1) | copy-done | bytes 131096
  2.1 0.0 copy-start.2
  2.1 0.8 copy-done.2
  2.9 0.0 copy-start.3
  2.9 0.7 copy-done.3
  3.6 81.6 %shard_map.46 = f32[16,160]{1,0:T(8,128)S(1)} custom-call(bf16[16,32,128]{2,1,0:T(8,128)(2,1)S(1)} %copy-done.1, bf16[64,64,128]{2,1,0:T(8,128)(2,1)S(1)} %copy-done, s32[16,160]{1,0:T(8,128)S(1)} %copy-done.3, s32[64,128]{1,0:T(8,128)S(1)} %bitcast.1), custom_call_target="tpu_custom_call" | custom-call | tf_op jit(solution)/shard_map/pallas_call | solution.py:163
  85.2 0.6 copy.6
Async XLA Ops:
  0.0 1.2 %copy-start = (bf16[64,64,128]{2,1,0:T(8,128)(2,1)S(1)}, bf16[64,64,128]{2,1,0:T(8,128)(2,1)}, u32[]{:S(2)}) copy-start(bf16[64,64,128]{2,1,0:T(8,128)(2,1)} %p_ref.1) | copy-start | bytes 3145732
  1.2 0.9 %copy-start.1 = (bf16[16,32,128]{2,1,0:T(8,128)(2,1)S(1)}, bf16[16,32,128]{2,1,0:T(8,128)(2,1)}, u32[]{:S(2)}) copy-start(bf16[16,32,128]{2,1,0:T(8,128)(2,1)} %q_ref.1) | copy-start | bytes 393220
  2.1 0.8 copy-start.2
  2.9 0.7 copy-start.3

commit v2 on v1

--- a/solution.py
+++ b/solution.py
@@ -12,32 +12,53 @@
 CAP = 3
 PEERS = 128
 CHUNK = 16
+WINDOW = 8
 MESH = pl.DeviceIdType.MESH
 
 
 def offset_target(y, c, z, x, o, sign):
-    i, j = o // 32, (o // 8) % 4
-    dx, dc = (o // 2) % 4, o % 2
-    dz = (j % 2) * 2 + j // 2
-    dy = (i + dz + dx) % 4
-    ty = (y + sign * dy + 4) % 4
-    tz = (z + sign * dz + 4) % 4
-    tx = (x + sign * dx + 4) % 4
-    tc = (c + dc) % 2
+    o = (o * 27) & 127
+    i, j, dx, dc = o >> 5, (o >> 3) & 3, (o >> 1) & 3, o & 1
+    dz = ((j & 1) << 1) + (j >> 1)
+    dy = (i + dz + dx) & 3
+    ty, tz, tx, tc = (y + sign * dy) & 3, (z + sign * dz) & 3, (x + sign * dx) & 3, (c + dc) & 1
     group, shard = ty * 2 + tc, tz * 4 + tx
     return group, shard, group * 16 + shard
 
 
 def kernel(
-    q_ref, p_ref, cand_ref, slot_ref, out_ref,
-    send, recv, pt, p32, retsend, ret, picked, route, route_s,
-    send_sem, recv_sem, retsend_sem, ret_sem, local_sem,
+    q_hbm, p_hbm, cand_hbm, slot_hbm, out_ref,
+    q_ref, p_ref, cand_ref, slot_ref, send, recv, pt, p32, retsend, ret, picked, route, route_s,
+    send_sem, recv_sem, retsend_sem, ret_sem, local_sem, in_sem, ready,
 ):
     group, shard = lax.axis_index("group"), lax.axis_index("shard")
     y, c, z, x = group // 2, group % 2, shard // 4, shard % 4
     me = group * 16 + shard
     qn, tok, dim = q_ref.shape
     rows = CAP * tok
+
+    inputs = [
+        pltpu.make_async_copy(src, dst, in_sem.at[i])
+        for i, (src, dst) in enumerate(
+            ((cand_hbm, cand_ref), (slot_hbm, slot_ref), (q_hbm, q_ref), (p_hbm, p_ref)))
+    ]
+    for copy in inputs:
+        copy.start()
+    barrier = pltpu.get_barrier_semaphore()
+
+    along_x = [(group, z * 4 + ((x + d) & 3)) for d in (1, 2, 3)]
+    along_y = [(((y + d) & 3) * 2 + c, shard) for d in (1, 2, 3)]
+    along_z = [(group, ((z + d) & 3) * 4 + x) for d in (1, 2, 3)]
+    other = [(group + 1 - 2 * c, shard)]
+
+    def tell(peers, sem):
+        for peer in peers:
+            pl.semaphore_signal(sem, inc=1, device_id=peer, device_id_type=MESH)
+
+    tell(along_z + along_y + along_x + other, barrier)
+
+    inputs[0].wait()
+    inputs[1].wait()
 
     cand = cand_ref[...]
     wide = jnp.concatenate(
@@ -74,21 +95,38 @@
         for r in range(CAP):
             ref[pl.ds(o * rows + r * tok, tok), :] = q_ref[route_s[r, number]]
 
+    inputs[2].wait()
     fill(recv, 0, me)
 
     @pl.loop(1, PEERS)
     def _(o):
-        tg, ts, number = offset_target(y, c, z, x, o, 1)
+        _, _, number = offset_target(y, c, z, x, o, 1)
         fill(send, o, number)
-        pltpu.make_async_remote_copy(
-            src_ref=send.at[pl.ds(o * rows, rows), :],
-            dst_ref=recv.at[pl.ds(o * rows, rows), :],
-            send_sem=send_sem,
-            recv_sem=recv_sem.at[o // CHUNK],
-            device_id=(tg, ts),
-            device_id_type=MESH,
-        ).start()
-
+
+    pl.semaphore_wait(barrier, 10)
+    for i, peers in enumerate((along_y, along_z, other)):
+        tell(peers, ready.at[i])
+        pl.semaphore_wait(ready.at[i], len(peers))
+
+    def launch(k, first):
+        @pl.loop(first, CHUNK)
+        def _(j):
+            o = k * CHUNK + j
+            tg, ts, _ = offset_target(y, c, z, x, o, 1)
+            pltpu.make_async_remote_copy(
+                src_ref=send.at[pl.ds(o * rows, rows), :],
+                dst_ref=recv.at[pl.ds(o * rows, rows), :],
+                send_sem=send_sem,
+                recv_sem=recv_sem.at[k],
+                device_id=(tg, ts),
+                device_id_type=MESH,
+            ).start()
+
+    launch(0, 1)
+    for k in range(1, WINDOW):
+        launch(k, 0)
+
+    inputs[3].wait()
     p32[...] = p_ref[...].reshape(p32.shape).astype(jnp.float32)
     for t in range(64):
         pt[t * 64:(t + 1) * 64, :] = p32[pl.ds(t, 64, stride=64), :].astype(jnp.bfloat16)
@@ -117,6 +155,10 @@
             part = recv.at[pl.ds(k * CHUNK * rows, CHUNK * rows), :]
             pltpu.make_async_copy(part, part, recv_sem.at[k]).wait()
 
+        @pl.when(k + WINDOW < PEERS // CHUNK)
+        def _():
+            launch(k + WINDOW, 0)
+
         total = score(k)
         for j in range(CHUNK):
             retsend[k * CHUNK + j, 0:CAP, :] = total[j * CAP:(j + 1) * CAP, :]
@@ -163,9 +205,13 @@
     return pl.pallas_call(
         kernel,
         out_shape=jax.ShapeDtypeStruct(candidates.shape, jnp.float32),
-        in_specs=[pl.BlockSpec(memory_space=pltpu.VMEM)] * 4,
+        in_specs=[pl.BlockSpec(memory_space=pl.ANY)] * 4,
         out_specs=pl.BlockSpec(memory_space=pltpu.VMEM),
         scratch_shapes=[
+            pltpu.VMEM(queries.shape, queries.dtype),
+            pltpu.VMEM(passages.shape, passages.dtype),
+            pltpu.VMEM(candidates.shape, candidates.dtype),
+            pltpu.VMEM((64, 128), jnp.int32),
             pltpu.VMEM((PEERS * rows, dim), jnp.bfloat16),
             pltpu.VMEM((PEERS * rows, dim), jnp.bfloat16),
             pltpu.VMEM((4096, dim), jnp.bfloat16),
@@ -180,9 +226,11 @@
             pltpu.SemaphoreType.DMA,
             pltpu.SemaphoreType.DMA,
             pltpu.SemaphoreType.DMA,
+            pltpu.SemaphoreType.DMA((4,)),
+            pltpu.SemaphoreType.REGULAR((3,)),
         ],
         compiler_params=pltpu.CompilerParams(
-            has_side_effects=True, vmem_limit_bytes=52 * 2**20),
+            collective_id=0, has_side_effects=True, vmem_limit_bytes=62 * 2**20),
     )(queries, passages, candidates, passage_slot.reshape(64, 128))
 
 

time: 86.1 us -> 65.3 us (0.76)
  Pallas kernels: 81.6 us -> 63.7 us
  local copies, waits for them, and re-layouts: 4.21 us -> 1.32 us
    pallas_call x1, Pallas kernels: 81.6 us -> 63.7 us  [local(): pl.pallas_call(kernel, out_shape=jax.ShapeDtypeStruct(candidates.shape, j...]
    unnamed x9 -> x1, local copies, waits for them, and re-layouts: 4.21 us -> 1.32 us
where the time goes in v2:
time: 65.3 us; the launch traced here: 65.1 us
  Pallas kernels  63.7 us (98%)
  local copies, waits for them, and re-layouts  1.32 us (2%)
    pallas_call x1, Pallas kernels, local(): pl.pallas_call(kernel, out_shape=jax.ShapeDtypeStruct(candidates.shape, j...  63.7 us
    unnamed x1, local copies, waits for them, and re-layouts  1.32 us

profile of v2, /device:TPU:1, one launch (start us, length us, event | category | flops | bytes accessed | tf_op | source)
XLA Modules:
  0.0 65.1 jit_solution(11915539918015034570)
XLA Ops:
  0.0 63.7 %shard_map.46 = f32[16,160]{1,0:T(8,128)} custom-call(bf16[16,32,128]{2,1,0:T(8,128)(2,1)} %q_hbm.1, bf16[64,64,128]{2,1,0:T(8,128)(2,1)} %p_hbm.1, s32[16,160]{1,0:T(8,128)} %cand_hbm.1, s32[64,128]{1,0:T(8,128)} %bitcast.1), custom_call_target="tpu_custom_call" | custom-call | tf_op jit(solution)/shard_map/pallas_call | solution.py:205
  63.8 1.3 %copy.6 = f32[16,160]{1,0:T(8,128)} copy(f32[16,160]{1,0:T(8,128)} %shard_map.46) | data formatting | bytes 20480

commit v3 on v1

v3 whole, which is shorter than its diff:
```python
import functools

import jax
import jax.numpy as jnp
from jax import lax
from jax.experimental import pallas as pl
from jax.experimental.pallas import tpu as pltpu
from jax.sharding import PartitionSpec as P

PER_VISIT = 20
SPREAD = 8
CAP = 3
PEERS = 128
CHUNK = 8
DIRECT = 24
EARLY = 2
QUEUED = 64
MESH = pl.DeviceIdType.MESH


def order():
    chips = [(0, 0, 0)]
    for d in (1, 2, 3):
        chips += [(d, 0, 0), (0, d, 0), (0, 0, d)]
    for m in range(9):
        p, q = m % 3 + 1, (m % 3 + m // 3) % 3 + 1
        chips += [(p, 0, q), (q, p, 0), (0, q, p)]
    for m in range(27):
        u, v, w = m % 3, m // 3 % 3, m // 9
        chips.append((u + 1, (u + v) % 3 + 1, (u + w) % 3 + 1))
    return [chip + (core,) for chip in chips for core in (0, 1)]


def passed_by(ahead):
    axes = [i for i in range(3) if ahead[i]]
    if len(axes) == 2:
        first = 2 if axes == [0, 2] else axes[0]
        second = sum(axes) - first
        return second if ahead[second] == 2 and ahead[first] != 2 else first
    for i in range(3):
        if ahead[i] == 2 and ahead[(i + 1) % 3] != 2:
            return i
    return sum(d == 3 for d in ahead[:3]) % 3


def kernel(
    q_hbm, p_hbm, cand_hbm, slot_hbm, out_ref,
    q_ref, p_ref, cand_ref, slot_ref, near_q, near_route, near_route_s, peer_s, send, recv, pt, p32, retsend, ret, picked, route, route_s,
    send_sem, recv_sem, retsend_sem, ret_sem, local_sem, in_sem, ready, near_sem,
):
    group, shard = lax.axis_index("group"), lax.axis_index("shard")
    y, c, z, x = group // 2, group % 2, shard // 4, shard % 4
    me = group * 16 + shard
    qn, tok, dim = q_ref.shape
    rows = CAP * tok

    inputs = [
        pltpu.make_async_copy(src, dst, in_sem.at[i])
        for i, (src, dst) in enumerate(
            ((cand_hbm, cand_ref), (slot_hbm, slot_ref), (q_hbm, q_ref), (p_hbm, p_ref)))
    ]
    for copy in inputs:
        copy.start()
    barrier = pltpu.get_barrier_semaphore()

    lines = [
        peer
        for d in (1, 2, 3)
        for peer in ((group, z * 4 + ((x + d) & 3)), (((y + d) & 3) * 2 + c, shard), (group, ((z + d) & 3) * 4 + x))
    ]
    flip = 1 - 2 * c
    chips = [(group + flip, shard)] + [(g + flip, h) for g, h in lines]

    def tell(peers, sem):
        for peer in peers:
            pl.semaphore_signal(sem, inc=1, device_id=peer, device_id_type=MESH)

    tell(lines + chips, barrier)

    inputs[0].wait()
    inputs[1].wait()

    cand = cand_ref[...]
    wide = jnp.concatenate(
        [jnp.pad(cand[:, k * PER_VISIT:(k + 1) * PER_VISIT], ((0, 0), (0, 128 - PER_VISIT)))
         for k in range(SPREAD)], axis=0)
    cand_t = wide.T[:24]
    hi, lo = cand_t // 128, cand_t % 128
    storage = jnp.zeros((24, 128), jnp.int32)
    for h in range(64):
        line = jnp.broadcast_to(slot_ref[h:h + 1, :], (24, 128))
        storage = jnp.where(hi == h, jnp.take_along_axis(line, lo, axis=1), storage)
    target = storage[0:1, :] // 64

    down = lax.broadcasted_iota(jnp.int32, (128, 128), 0)
    across = lax.broadcasted_iota(jnp.int32, (128, 128), 1)
    matches = down == target
    matches_b = jnp.where(matches, 1.0, 0.0).astype(jnp.bfloat16)
    upper = jnp.where(down < across, 1.0, 0.0).astype(jnp.bfloat16)
    before = jnp.dot(matches_b, upper, preferred_element_type=jnp.float32)
    rank = jnp.sum(jnp.where(matches, before, 0.0), axis=0, keepdims=True)
    place = storage % 64 + jnp.where(rank == 1.0, 64, 0)
    place = jnp.pad(place, ((0, 104), (0, 0))).T
    query = (lax.broadcasted_iota(jnp.int32, (8, 128), 1) % qn).astype(jnp.float32)
    level = lax.broadcasted_iota(jnp.int32, (8, 128), 0).astype(jnp.float32)
    held = jnp.where(level == rank, query, 0.0).astype(jnp.bfloat16)
    slots = lax.dot_general(held, matches_b, (((1,), (1,)), ((), ())), preferred_element_type=jnp.float32)
    route[0:8, :] = jnp.clip(slots.astype(jnp.int32), 0, qn - 1)
    route[8:16, :] = jnp.broadcast_to(jnp.clip(target, 0, PEERS - 1), (8, 128))
    route[16:24, :] = jnp.broadcast_to(jnp.where(rank > 1.0, 1, 0), (8, 128))
    copy = pltpu.make_async_copy(route, route_s, local_sem)
    copy.start()
    copy.wait()

    ahead_y = [[(((y + d) & 3) * 2 + ((c + e) & 1)) for e in (0, 1)] for d in range(4)]
    ahead_zx = [[((z + d) & 3) * 4 + ((x + e) & 3) for e in range(4)] for d in range(4)]
    for o, (dx, dy, dz, dc) in enumerate(order()):
        peer_s[0, o] = ahead_y[-dy % 4][dc]
        peer_s[1, o] = ahead_zx[-dz % 4][-dx % 4]
        if o >= DIRECT:
            axis = passed_by((dx, dy, dz))
            by = (dx, dy, dz)[axis]
            dx, dy, dz = (0 if i == axis else d for i, d in enumerate((dx, dy, dz)))
            peer_s[4, o] = axis * 3 + by - 1
        peer_s[2, o] = ahead_y[dy][dc]
        peer_s[3, o] = ahead_zx[dz][dx]

    def fill(ref, o, number):
        for r in range(CAP):
            ref[pl.ds(o * rows + r * tok, tok), :] = q_ref[route_s[r, number]]

    def fill_near(o):
        line, number = peer_s[4, o], peer_s[2, o] * 16 + peer_s[3, o]
        for r in range(CAP):
            send[pl.ds(o * rows + r * tok, tok), :] = near_q[line * qn + near_route_s[line * 8 + r, number]]

    inputs[2].wait()
    fill(recv, 0, me)

    @pl.loop(1, DIRECT)
    def _(o):
        fill(send, o, peer_s[2, o] * 16 + peer_s[3, o])

    def start(o):
        pltpu.make_async_remote_copy(
            src_ref=send.at[pl.ds(o * rows, rows), :],
            dst_ref=recv.at[pl.ds(o * rows, rows), :],
            send_sem=send_sem,
            recv_sem=recv_sem.at[o // CHUNK],
            device_id=(peer_s[2, o], peer_s[3, o]),
            device_id_type=MESH,
        ).start()

    def launch(first, end):
        @pl.loop(first, end)
        def _(o):
            start(o)

    def launch_near(first):
        for j in range(CHUNK):
            fill_near(first + j)
            start(first + j)

    pl.semaphore_wait(barrier, 19)
    tell(lines, ready.at[0])
    launch(1, 20)
    for d in (1, 2, 3):
        for axis in range(3):
            line, peer = axis * 3 + d - 1, lines[(d - 1) * 3 + axis]
            pltpu.make_async_remote_copy(
                src_ref=route.at[pl.ds(0, 8), :], dst_ref=near_route.at[pl.ds(line * 8, 8), :],
                send_sem=near_sem.at[0], recv_sem=near_sem.at[1], device_id=peer, device_id_type=MESH).start()
            pltpu.make_async_remote_copy(
                src_ref=q_ref, dst_ref=near_q.at[pl.ds(line * qn, qn)],
                send_sem=near_sem.at[2], recv_sem=near_sem.at[3], device_id=peer, device_id_type=MESH).start()
    pl.semaphore_wait(ready.at[0], 9)
    tell(lines, ready.at[1])
    launch(20, DIRECT)

    inputs[3].wait()
    p32[...] = p_ref[...].reshape(p32.shape).astype(jnp.float32)
    for t in range(64):
        pt[t * 64:(t + 1) * 64, :] = p32[pl.ds(t, 64, stride=64), :].astype(jnp.bfloat16)

    def score(k):
        lhs = recv[pl.ds(k * CHUNK * rows, CHUNK * rows), :]
        best = None
        for n in range(16):
            sim = lax.dot_general(
                lhs, pt[n * 256:(n + 1) * 256, :], (((1,), (1,)), ((), ())),
                preferred_element_type=jnp.float32)
            two = jnp.maximum(sim[:, :128], sim[:, 128:])
            best = two if best is None else jnp.maximum(best, two)
        best = jnp.maximum(best, pltpu.roll(best, 64, 1))
        return jnp.sum(best.reshape(CHUNK * CAP, tok, 128), axis=1) * (1.0 / tok)

    def step(k):
        @pl.when(k == 0)
        def _():
            part = recv.at[pl.ds(rows, (CHUNK - 1) * rows), :]
            pltpu.make_async_copy(part, part, recv_sem.at[0]).wait()

        @pl.when(k > 0)
        def _():
            part = recv.at[pl.ds(k * CHUNK * rows, CHUNK * rows), :]
            pltpu.make_async_copy(part, part, recv_sem.at[k]).wait()

        total = score(k)
        low = lax.broadcasted_iota(jnp.int32, (1, 128), 1) < 64
        for j in range(CHUNK):
            first, second, last = (total[j * CAP + r:j * CAP + r + 1, :] for r in range(CAP))
            retsend[k * CHUNK + j, 0:1, :] = jnp.where(low, first, second)
            retsend[k * CHUNK + j, 1:2, :] = last

        for j in range(CHUNK):
            o = k * CHUNK + j

            def answer():
                pltpu.make_async_remote_copy(
                    src_ref=retsend.at[o],
                    dst_ref=ret.at[me],
                    send_sem=retsend_sem,
                    recv_sem=ret_sem,
                    device_id=(peer_s[0, o], peer_s[1, o]),
                    device_id_type=MESH,
                ).start()

            if j:
                answer()
            else:
                pl.when(k > 0)(answer)

    @pl.loop(0, EARLY)
    def _(k):
        step(k)

    pltpu.make_async_copy(near_route, near_route, near_sem.at[1]).wait()
    copy = pltpu.make_async_copy(near_route, near_route_s, local_sem)
    copy.start()
    copy.wait()
    pltpu.make_async_copy(near_q, near_q, near_sem.at[3]).wait()

    @pl.loop(DIRECT // CHUNK, QUEUED // CHUNK)
    def _(i):
        launch_near(i * CHUNK)

    pl.semaphore_wait(ready.at[1], 9)

    @pl.loop(EARLY, PEERS // CHUNK)
    def _(k):
        after = k - EARLY + QUEUED // CHUNK

        @pl.when(after < PEERS // CHUNK)
        def _():
            launch_near(after * CHUNK)

        step(k)

    part = retsend.at[pl.ds(1, PEERS - 1)]
    pltpu.make_async_copy(part, part, ret_sem).wait()

    ret[me] = retsend[0]

    @pl.loop(0, PEERS, unroll=8)
    def _(v):
        picked[pl.ds(v, 1), :] = ret[route_s[8, v], pl.ds(route_s[16, v], 1), :]

    scores = jnp.take_along_axis(picked[...], place, axis=1)
    for k in range(SPREAD):
        out_ref[:, k * PER_VISIT:(k + 1) * PER_VISIT] = scores[k * qn:(k + 1) * qn, :PER_VISIT]

    pltpu.make_async_copy(part, part, retsend_sem).wait()
    pltpu.make_async_copy(near_route, near_route, near_sem.at[0]).wait()
    pltpu.make_async_copy(near_q, near_q, near_sem.at[2]).wait()
    part = send.at[pl.ds(rows, (PEERS - 1) * rows), :]
    pltpu.make_async_copy(part, part, send_sem).wait()


def local(queries, passages, candidates, passage_slot):
    rows = CAP * queries.shape[1]
    dim = queries.shape[2]
    return pl.pallas_call(
        kernel,
        out_shape=jax.ShapeDtypeStruct(candidates.shape, jnp.float32),
        in_specs=[pl.BlockSpec(memory_space=pl.ANY)] * 4,
        out_specs=pl.BlockSpec(memory_space=pltpu.VMEM),
        scratch_shapes=[
            pltpu.VMEM(queries.shape, queries.dtype),
            pltpu.VMEM(passages.shape, passages.dtype),
            pltpu.VMEM(candidates.shape, candidates.dtype),
            pltpu.VMEM((64, 128), jnp.int32),
            pltpu.VMEM((9 * queries.shape[0],) + queries.shape[1:], queries.dtype),
            pltpu.VMEM((72, 128), jnp.int32),
            pltpu.SMEM((72, 128), jnp.int32),
            pltpu.SMEM((8, 128), jnp.int32),
            pltpu.VMEM((PEERS * rows, dim), jnp.bfloat16),
            pltpu.VMEM((PEERS * rows, dim), jnp.bfloat16),
            pltpu.VMEM((4096, dim), jnp.bfloat16),
            pltpu.VMEM((4096, dim), jnp.float32),
            pltpu.VMEM((PEERS, 2, 128), jnp.float32),
            pltpu.VMEM((PEERS, 2, 128), jnp.float32),
            pltpu.VMEM((PEERS, 128), jnp.float32),
            pltpu.VMEM((24, 128), jnp.int32),
            pltpu.SMEM((24, 128), jnp.int32),
            pltpu.SemaphoreType.DMA,
            pltpu.SemaphoreType.DMA((PEERS // CHUNK,)),
            pltpu.SemaphoreType.DMA,
            pltpu.SemaphoreType.DMA,
            pltpu.SemaphoreType.DMA,
            pltpu.SemaphoreType.DMA((4,)),
            pltpu.SemaphoreType.REGULAR((2,)),
            pltpu.SemaphoreType.DMA((4,)),
        ],
        compiler_params=pltpu.CompilerParams(
            collective_id=0, has_side_effects=True, vmem_limit_bytes=62 * 2**20),
    )(queries, passages, candidates, passage_slot.reshape(64, 128))


def solution(mesh):
    return jax.shard_map(
        local,
        mesh=mesh,
        in_specs=(
            P(("group", "shard"), None, None),
            P(("group", "shard"), None, None),
            P(("group", "shard"), None),
            P(),
        ),
        out_specs=P(("group", "shard"), None),
        check_vma=False,
    )
```

time: 86.1 us -> 60.4 us (0.70)
  Pallas kernels: 81.6 us -> 58.8 us
  local copies, waits for them, and re-layouts: 4.21 us -> 1.32 us
    pallas_call x1, Pallas kernels: 81.6 us -> 58.8 us  [local(): pl.pallas_call(kernel, out_shape=jax.ShapeDtypeStruct(candidates.shape, j...]
    unnamed x9 -> x1, local copies, waits for them, and re-layouts: 4.21 us -> 1.32 us
where the time goes in v3:
time: 60.4 us; the launch traced here: 60.1 us
  Pallas kernels  58.8 us (97%)
  local copies, waits for them, and re-layouts  1.32 us (2%)
    pallas_call x1, Pallas kernels, local(): pl.pallas_call(kernel, out_shape=jax.ShapeDtypeStruct(candidates.shape, j...  58.8 us
    unnamed x1, local copies, waits for them, and re-layouts  1.32 us

profile of v3, /device:TPU:1, one launch (start us, length us, event | category | flops | bytes accessed | tf_op | source)
XLA Modules:
  0.0 60.1 jit_solution(4345806207358778990)
XLA Ops:
  0.0 58.8 %shard_map.46 = f32[16,160]{1,0:T(8,128)} custom-call(bf16[16,32,128]{2,1,0:T(8,128)(2,1)} %q_hbm.1, bf16[64,64,128]{2,1,0:T(8,128)(2,1)} %p_hbm.1, s32[16,160]{1,0:T(8,128)} %cand_hbm.1, s32[64,128]{1,0:T(8,128)} %bitcast.1), custom_call_target="tpu_custom_call" | custom-call | tf_op jit(solution)/shard_map/pallas_call | solution.py:282
  58.8 1.3 %copy.6 = f32[16,160]{1,0:T(8,128)} copy(f32[16,160]{1,0:T(8,128)} %shard_map.46) | data formatting | bytes 20480

commit v4 on v3

--- a/solution.py
+++ b/solution.py
@@ -15,6 +15,8 @@
 DIRECT = 24
 EARLY = 2
 QUEUED = 64
+WIDE = 1
+LATE = 0
 MESH = pl.DeviceIdType.MESH
 
 
@@ -25,9 +27,11 @@
     for m in range(9):
         p, q = m % 3 + 1, (m % 3 + m // 3) % 3 + 1
         chips += [(p, 0, q), (q, p, 0), (0, q, p)]
+    far = []
     for m in range(27):
         u, v, w = m % 3, m // 3 % 3, m // 9
-        chips.append((u + 1, (u + v) % 3 + 1, (u + w) % 3 + 1))
+        far.append((u + 1, (u + v) % 3 + 1, (u + w) % 3 + 1))
+    chips += sorted(far, key=lambda chip: -chip.count(2))
     return [chip + (core,) for chip in chips for core in (0, 1)]
 
 
@@ -77,6 +81,16 @@
 
     tell(lines + chips, barrier)
 
+    def pass_on(line, peer, queries):
+        src, dst = (q_ref, near_q.at[pl.ds(line * qn, qn)]) if queries else (
+            route.at[pl.ds(0, 8), :], near_route.at[pl.ds(line * 8, 8), :])
+        pltpu.make_async_remote_copy(
+            src_ref=src, dst_ref=dst, send_sem=near_sem.at[2 * queries], recv_sem=near_sem.at[2 * queries + 1],
+            device_id=peer, device_id_type=MESH).start()
+
+    inputs[2].wait()
+    pl.semaphore_wait(barrier, 19)
+    tell(lines, ready.at[0])
     inputs[0].wait()
     inputs[1].wait()
 
@@ -112,78 +126,66 @@
     copy.start()
     copy.wait()
 
-    ahead_y = [[(((y + d) & 3) * 2 + ((c + e) & 1)) for e in (0, 1)] for d in range(4)]
-    ahead_zx = [[((z + d) & 3) * 4 + ((x + e) & 3) for e in range(4)] for d in range(4)]
-    for o, (dx, dy, dz, dc) in enumerate(order()):
-        peer_s[0, o] = ahead_y[-dy % 4][dc]
-        peer_s[1, o] = ahead_zx[-dz % 4][-dx % 4]
-        if o >= DIRECT:
-            axis = passed_by((dx, dy, dz))
-            by = (dx, dy, dz)[axis]
-            dx, dy, dz = (0 if i == axis else d for i, d in enumerate((dx, dy, dz)))
-            peer_s[4, o] = axis * 3 + by - 1
-        peer_s[2, o] = ahead_y[dy][dc]
-        peer_s[3, o] = ahead_zx[dz][dx]
-
     def fill(ref, o, number):
         for r in range(CAP):
             ref[pl.ds(o * rows + r * tok, tok), :] = q_ref[route_s[r, number]]
 
-    def fill_near(o):
-        line, number = peer_s[4, o], peer_s[2, o] * 16 + peer_s[3, o]
-        for r in range(CAP):
-            send[pl.ds(o * rows + r * tok, tok), :] = near_q[line * qn + near_route_s[line * 8 + r, number]]
-
-    inputs[2].wait()
-    fill(recv, 0, me)
-
-    @pl.loop(1, DIRECT)
-    def _(o):
-        fill(send, o, peer_s[2, o] * 16 + peer_s[3, o])
-
-    def start(o):
+    ahead_y = [[(((y + d) & 3) * 2 + ((c + e) & 1)) for e in (0, 1)] for d in range(4)]
+    ahead_zx = [[((z + d) & 3) * 4 + ((x + e) & 3) for e in range(4)] for d in range(4)]
+    def start(o, group, shard):
         pltpu.make_async_remote_copy(
             src_ref=send.at[pl.ds(o * rows, rows), :],
             dst_ref=recv.at[pl.ds(o * rows, rows), :],
             send_sem=send_sem,
             recv_sem=recv_sem.at[o // CHUNK],
-            device_id=(peer_s[2, o], peer_s[3, o]),
+            device_id=(group, shard),
             device_id_type=MESH,
         ).start()
 
-    def launch(first, end):
-        @pl.loop(first, end)
-        def _(o):
-            start(o)
+    def direct(first, end):
+        for o, (dx, dy, dz, dc) in enumerate(order()):
+            if first <= o < end:
+                tg, ts = ahead_y[dy][dc], ahead_zx[dz][dx]
+                fill(send, o, tg * 16 + ts)
+                start(o, tg, ts)
+
+    fill(recv, 0, me)
+    direct(1, 20)
+    for d in (1, 2, 3):
+        for axis in range(3):
+            line, peer = axis * 3 + d - 1, lines[(d - 1) * 3 + axis]
+            pass_on(line, peer, 0)
+            pass_on(line, peer, 1)
+
+    def write_peers():
+        for o, (dx, dy, dz, dc) in enumerate(order()):
+            peer_s[0, o] = ahead_y[-dy % 4][dc]
+            peer_s[1, o] = ahead_zx[-dz % 4][-dx % 4]
+            if o >= DIRECT:
+                axis = passed_by((dx, dy, dz))
+                by = (dx, dy, dz)[axis]
+                dx, dy, dz = (0 if i == axis else d for i, d in enumerate((dx, dy, dz)))
+                peer_s[4, o] = axis * 3 + by - 1
+            peer_s[2, o] = ahead_y[dy][dc]
+            peer_s[3, o] = ahead_zx[dz][dx]
+
+    def fill_near(o):
+        line, number = peer_s[4, o], peer_s[2, o] * 16 + peer_s[3, o]
+        for r in range(CAP):
+            send[pl.ds(o * rows + r * tok, tok), :] = near_q[line * qn + near_route_s[line * 8 + r, number]]
 
     def launch_near(first):
         for j in range(CHUNK):
             fill_near(first + j)
-            start(first + j)
-
-    pl.semaphore_wait(barrier, 19)
-    tell(lines, ready.at[0])
-    launch(1, 20)
-    for d in (1, 2, 3):
-        for axis in range(3):
-            line, peer = axis * 3 + d - 1, lines[(d - 1) * 3 + axis]
-            pltpu.make_async_remote_copy(
-                src_ref=route.at[pl.ds(0, 8), :], dst_ref=near_route.at[pl.ds(line * 8, 8), :],
-                send_sem=near_sem.at[0], recv_sem=near_sem.at[1], device_id=peer, device_id_type=MESH).start()
-            pltpu.make_async_remote_copy(
-                src_ref=q_ref, dst_ref=near_q.at[pl.ds(line * qn, qn)],
-                send_sem=near_sem.at[2], recv_sem=near_sem.at[3], device_id=peer, device_id_type=MESH).start()
-    pl.semaphore_wait(ready.at[0], 9)
-    tell(lines, ready.at[1])
-    launch(20, DIRECT)
+            start(first + j, peer_s[2, first + j], peer_s[3, first + j])
 
     inputs[3].wait()
     p32[...] = p_ref[...].reshape(p32.shape).astype(jnp.float32)
     for t in range(64):
         pt[t * 64:(t + 1) * 64, :] = p32[pl.ds(t, 64, stride=64), :].astype(jnp.bfloat16)
 
-    def score(k):
-        lhs = recv[pl.ds(k * CHUNK * rows, CHUNK * rows), :]
+    def score(first, size):
+        lhs = recv[pl.ds(first * rows, size * rows), :]
         best = None
         for n in range(16):
             sim = lax.dot_general(
@@ -192,47 +194,42 @@
             two = jnp.maximum(sim[:, :128], sim[:, 128:])
             best = two if best is None else jnp.maximum(best, two)
         best = jnp.maximum(best, pltpu.roll(best, 64, 1))
-        return jnp.sum(best.reshape(CHUNK * CAP, tok, 128), axis=1) * (1.0 / tok)
-
-    def step(k):
-        @pl.when(k == 0)
-        def _():
-            part = recv.at[pl.ds(rows, (CHUNK - 1) * rows), :]
-            pltpu.make_async_copy(part, part, recv_sem.at[0]).wait()
-
-        @pl.when(k > 0)
-        def _():
-            part = recv.at[pl.ds(k * CHUNK * rows, CHUNK * rows), :]
-            pltpu.make_async_copy(part, part, recv_sem.at[k]).wait()
-
-        total = score(k)
-        low = lax.broadcasted_iota(jnp.int32, (1, 128), 1) < 64
-        for j in range(CHUNK):
-            first, second, last = (total[j * CAP + r:j * CAP + r + 1, :] for r in range(CAP))
-            retsend[k * CHUNK + j, 0:1, :] = jnp.where(low, first, second)
-            retsend[k * CHUNK + j, 1:2, :] = last
-
-        for j in range(CHUNK):
-            o = k * CHUNK + j
-
-            def answer():
-                pltpu.make_async_remote_copy(
-                    src_ref=retsend.at[o],
-                    dst_ref=ret.at[me],
-                    send_sem=retsend_sem,
-                    recv_sem=ret_sem,
-                    device_id=(peer_s[0, o], peer_s[1, o]),
-                    device_id_type=MESH,
-                ).start()
-
-            if j:
-                answer()
-            else:
-                pl.when(k > 0)(answer)
-
-    @pl.loop(0, EARLY)
-    def _(k):
-        step(k)
+        return jnp.sum(best.reshape(size * CAP, tok, 128), axis=1) * (1.0 / tok)
+
+    low = lax.broadcasted_iota(jnp.int32, (1, 128), 1) < 64
+
+    def arrive(group, skip=0):
+        part = recv.at[pl.ds((group * CHUNK + skip) * rows, (CHUNK - skip) * rows), :]
+        pltpu.make_async_copy(part, part, recv_sem.at[group]).wait()
+
+    def step(group, groups, own=False, peers=None, beside=None):
+        for g in range(groups):
+            arrive(group + g, 1 if own and g == 0 else 0)
+        first, size = group * CHUNK, groups * CHUNK
+        if beside is not None:
+            beside()
+        total = score(first, size)
+        for j in range(size):
+            one, two, three = (total[j * CAP + r:j * CAP + r + 1, :] for r in range(CAP))
+            retsend[first + j, 0:1, :] = jnp.where(low, one, two)
+            retsend[first + j, 1:2, :] = three
+        for j in range(1 if own else 0, size):
+            pltpu.make_async_remote_copy(
+                src_ref=retsend.at[first + j],
+                dst_ref=ret.at[me],
+                send_sem=retsend_sem,
+                recv_sem=ret_sem,
+                device_id=peers[j] if peers else (peer_s[0, first + j], peer_s[1, first + j]),
+                device_id_type=MESH,
+            ).start()
+
+    behind = [(ahead_y[-dy % 4][dc], ahead_zx[-dz % 4][-dx % 4]) for dx, dy, dz, dc in order()[:EARLY * CHUNK]]
+    step(0, 1, own=True, peers=behind[:CHUNK], beside=write_peers)
+    pl.semaphore_wait(ready.at[0], 9)
+    tell(lines, ready.at[1])
+    direct(20, DIRECT)
+    for k in range(1, EARLY):
+        step(k, 1, peers=behind[k * CHUNK:(k + 1) * CHUNK])
 
     pltpu.make_async_copy(near_route, near_route, near_sem.at[1]).wait()
     copy = pltpu.make_async_copy(near_route, near_route_s, local_sem)
@@ -246,15 +243,23 @@
 
     pl.semaphore_wait(ready.at[1], 9)
 
-    @pl.loop(EARLY, PEERS // CHUNK)
-    def _(k):
-        after = k - EARLY + QUEUED // CHUNK
-
-        @pl.when(after < PEERS // CHUNK)
-        def _():
-            launch_near(after * CHUNK)
-
-        step(k)
+    steps = (PEERS // CHUNK - EARLY - LATE) // WIDE
+
+    @pl.loop(0, steps)
+    def _(i):
+        for g in range(WIDE):
+            after = QUEUED // CHUNK + i * WIDE + g
+
+            @pl.when(after < PEERS // CHUNK)
+            def _():
+                launch_near(after * CHUNK)
+
+        step(EARLY + i * WIDE, WIDE)
+
+    if LATE:
+        @pl.loop(PEERS // CHUNK - LATE, PEERS // CHUNK)
+        def _(i):
+            step(i, 1)
 
     part = retsend.at[pl.ds(1, PEERS - 1)]
     pltpu.make_async_copy(part, part, ret_sem).wait()

time: 60.4 us -> 58 us (0.960)
  Pallas kernels: 58.8 us -> 56.5 us
    pallas_call x1, Pallas kernels: 58.8 us -> 56.5 us  [local(): pl.pallas_call(kernel, out_shape=jax.ShapeDtypeStruct(candidates.shape, j...]
where the time goes in v4:
time: 58 us; the launch traced here: 57.8 us
  Pallas kernels  56.5 us (97%)
  local copies, waits for them, and re-layouts  1.32 us (2%)
    pallas_call x1, Pallas kernels, local(): pl.pallas_call(kernel, out_shape=jax.ShapeDtypeStruct(candidates.shape, j...  56.5 us
    unnamed x1, local copies, waits for them, and re-layouts  1.32 us

profile of v4, /device:TPU:1, one launch (start us, length us, event | category | flops | bytes accessed | tf_op | source)
XLA Modules:
  0.0 57.8 jit_solution(8462230627405674331)
XLA Ops:
  0.0 56.5 %shard_map.46 = f32[16,160]{1,0:T(8,128)} custom-call(bf16[16,32,128]{2,1,0:T(8,128)(2,1)} %q_hbm.1, bf16[64,64,128]{2,1,0:T(8,128)(2,1)} %p_hbm.1, s32[16,160]{1,0:T(8,128)} %cand_hbm.1, s32[64,128]{1,0:T(8,128)} %bitcast.1), custom_call_target="tpu_custom_call" | custom-call | tf_op jit(solution)/shard_map/pallas_call | solution.py:287
  56.5 1.3 %copy.6 = f32[16,160]{1,0:T(8,128)} copy(f32[16,160]{1,0:T(8,128)} %shard_map.46) | data formatting | bytes 20480

commit v5 on v4

--- a/solution.py
+++ b/solution.py
@@ -234,8 +234,8 @@
     pltpu.make_async_copy(near_route, near_route, near_sem.at[1]).wait()
     copy = pltpu.make_async_copy(near_route, near_route_s, local_sem)
     copy.start()
+    pltpu.make_async_copy(near_q, near_q, near_sem.at[3]).wait()
     copy.wait()
-    pltpu.make_async_copy(near_q, near_q, near_sem.at[3]).wait()
 
     @pl.loop(DIRECT // CHUNK, QUEUED // CHUNK)
     def _(i):

time: 58 us -> 58 us (level)
  no operation moved by 1% of the time
where the time goes in v5:
time: 58 us; the launch traced here: 57.8 us
  Pallas kernels  56.5 us (97%)
  local copies, waits for them, and re-layouts  1.32 us (2%)
    pallas_call x1, Pallas kernels, local(): pl.pallas_call(kernel, out_shape=jax.ShapeDtypeStruct(candidates.shape, j...  56.5 us
    unnamed x1, local copies, waits for them, and re-layouts  1.32 us

profile of v5, /device:TPU:1, one launch (start us, length us, event | category | flops | bytes accessed | tf_op | source)
XLA Modules:
  0.0 57.8 jit_solution(16692752897575766260)
XLA Ops:
  0.0 56.5 %shard_map.46 = f32[16,160]{1,0:T(8,128)} custom-call(bf16[16,32,128]{2,1,0:T(8,128)(2,1)} %q_hbm.1, bf16[64,64,128]{2,1,0:T(8,128)(2,1)} %p_hbm.1, s32[16,160]{1,0:T(8,128)} %cand_hbm.1, s32[64,128]{1,0:T(8,128)} %bitcast.1), custom_call_target="tpu_custom_call" | custom-call | tf_op jit(solution)/shard_map/pallas_call | solution.py:287
  56.5 1.3 %copy.6 = f32[16,160]{1,0:T(8,128)} copy(f32[16,160]{1,0:T(8,128)} %shard_map.46) | data formatting | bytes 20480
